TPU v7x, 256 devices: a whole 4x4x8 slice. The times are simulated.
256 devices in a mesh: expert: 16 (over x, z_lo, core), split: 16 (over z_hi, y).
Axes of the slice: x: 4, y: 4, z: 8 (z_hi: 4, z_lo: 2; z = z_hi * 2 + z_lo), core: 2. Of those that a mesh axis runs over, the one named last changes fastest.
Arguments:
- tokens: bfloat16 [4096, 3072], P('expert', 'split'), may hold values from -6 to 6
- expert_ids: int32 [4096, 2], P('expert'), may hold values from 0 to 15, all different within a row; in each aligned block of 256 rows (0 to 255, 256 to 511, ...) at most 64 rows name the same one
- pair_logits: float32 [4096, 2], P('expert'), may hold values from -6 to 6
- gate_weight: bfloat16 [16, 3072, 8192], P('expert', None, 'split'), may hold values from -0.109375 to 0.109375
- up_weight: bfloat16 [16, 3072, 8192], P('expert', None, 'split'), may hold values from -0.109375 to 0.109375
- down_weight: bfloat16 [16, 8192, 3072], P('expert', 'split'), may hold values from -0.0625 to 0.0625
Outputs:
- mixed: bfloat16 [4096, 3072], P('expert', 'split')
Inputs may be any that keep to these rules, and one draw needn't show every extreme that they name: `expert_ids`: the two experts of a token differ. Within each aligned block of 256 tokens (the tokens of one index of expert) no expert is named by more than 64 pairs, a bound that some block reaches.
All inputs are finite; a program needn't handle non-finite values.
Results may differ from a plain program's by a relative error of at most 0.019.
Values may be sent and summed in bfloat16 or wider, within the bound.
A program may use at most 64 MiB of HBM per device.

v0:
```python
import jax
import jax.numpy as jnp
from jax import lax
from jax.sharding import PartitionSpec as P


def body(tokens, expert_ids, pair_logits, gate_weight, up_weight, down_weight):
    experts = lax.axis_size("expert")
    tok_rows = tokens.shape[0]
    capacity = 4 * tok_rows // experts
    flat = expert_ids.reshape(-1)
    labels = jnp.arange(experts, dtype=jnp.int32)
    onehot = (flat[:, None] == labels[None, :]).astype(jnp.int32)
    before = jnp.cumsum(onehot, axis=0) - onehot
    slot = jnp.sum(before * onehot, axis=1)
    dest = flat * capacity + slot
    first = jax.nn.sigmoid(pair_logits[:, 0] - pair_logits[:, 1])
    mix = jnp.stack([first, 1.0 - first], axis=1).reshape(-1)
    w_gate = gate_weight[0]
    w_up = up_weight[0]
    w_down = down_weight[0]
    narrow = tokens.shape[1]
    select = (jnp.arange(experts * capacity, dtype=jnp.int32)[:, None] == dest[None, :]).astype(
        jnp.bfloat16
    )
    doubled = jnp.repeat(tokens, 2, axis=0)
    packed = jnp.dot(select, doubled, preferred_element_type=jnp.float32).astype(jnp.bfloat16)
    sending = packed.reshape(experts, capacity, narrow)
    arrived = lax.all_to_all(sending, "expert", split_axis=0, concat_axis=0, tiled=True).reshape(
        experts * capacity, narrow
    )
    piece = lax.all_gather(arrived, "split", axis=1, tiled=True)
    gate = jnp.dot(piece, w_gate, preferred_element_type=jnp.float32)
    up_part = jnp.dot(piece, w_up, preferred_element_type=jnp.float32)
    hidden = (jax.nn.silu(gate) * up_part).astype(jnp.bfloat16)
    terms = jnp.dot(hidden, w_down, preferred_element_type=jnp.float32)
    result = lax.psum_scatter(
        terms.astype(jnp.bfloat16), "split", scatter_dimension=1, tiled=True
    ).astype(jnp.float32)
    narrow = result.shape[1]
    returned = lax.all_to_all(
        result.reshape(experts, capacity, narrow).astype(jnp.bfloat16),
        "expert",
        split_axis=0,
        concat_axis=0,
        tiled=True,
    ).astype(jnp.float32)
    returned = returned.reshape(experts * capacity, narrow)
    picked = returned[dest] * mix[:, None]
    mixed = picked.reshape(tok_rows, 2, narrow).sum(axis=1)
    return mixed.astype(jnp.bfloat16)


def solution(mesh):
    in_specs = (
        P("expert", "split"),
        P("expert", None),
        P("expert", None),
        P("expert", None, "split"),
        P("expert", None, "split"),
        P("expert", "split", None),
    )
    out_specs = P("expert", "split")
    return jax.shard_map(body, mesh=mesh, in_specs=in_specs, out_specs=out_specs, check_vma=False)
```

profile of v0, /device:TPU:1, one launch (start us, length us, event | category | flops | bytes accessed | tf_op | source)
XLA Modules:
  0.0 293.0 jit_solution(6479677661209688101)
XLA Ops:
  6.5 0.0 copy-start
  6.5 0.0 all-gather.2.cloned.1.call-start
  6.5 1.0 copy.28
  7.5 0.1 eq.40
  7.7 0.1 reshape.81
  7.8 1.2 reduce-window.6
  9.0 0.2 slice_reduce_fusion
  9.2 0.1 fusion.15
  9.3 1.0 copy.31
  10.3 0.1 broadcast_in_dim.2
  10.5 0.9 reshape.83
  11.4 1.6 fusion.10
  13.0 1.0 copy.32
  14.0 17.2 %all_to_all.10 = bf16[16,64,192]{2,1,0:T(8,128)(2,1)} all-to-all(bf16[16,64,192]{2,1,0:T(8,128)(2,1)} %bitcast.44), channel_id=1, replica_groups=mesh['expert'=16,'split'=16] {'expert'}, dimensions={0} | all-to-all | bytes 786432 | tf_op jit(solution)/shard_map/all_to_all | solution.py:29
  31.2 2.0 copy.33
  33.2 0.0 all-gather.2.cloned.1.call-update
  33.2 0.0 reduce-scatter.2.cloned.1.call-start
  33.3 91.2 %all-gather.2.cloned.1.call-done = bf16[1024,3072]{0,1:T(8,128)(2,1)} async-done(((bf16[1024,192]{0,1:T(8,128)(2,1)}), bf16[1024,3072]{0,1:T(8,128)(2,1)}) %all-gather.2.cloned.1.call-update) | async-done | bytes 6291472 | tf_op jit(solution)/shard_map/all_gather | solution.py:32
  124.5 8.5 %fusion.1 = f32[1024,512]{1,0:T(8,128)} fusion(bf16[1024,3072]{0,1:T(8,128)(2,1)} %all-gather.2.cloned.1.call-done, bf16[1,3072,512]{2,1,0:T(8,128)(2,1)} %param.10), kind=kOutput, calls=%fused_computation.3 | convolution fusion | flops 3221225472 | bytes 11534336 | tf_op jit(solution)/shard_map/dot_general | solution.py:34
  133.0 0.0 copy-done
  133.0 12.5 %convolution_convert_fusion = bf16[1024,3072]{0,1:T(8,128)(2,1)} fusion(bf16[1,512,3072]{2,1,0:T(8,128)(2,1)S(1)} %copy-done, f32[1024,512]{1,0:T(8,128)} %fusion.1, bf16[1024,3072]{0,1:T(8,128)(2,1)} %all-gather.2.cloned.1.call-done, bf16[1,3072,512]{2,1,0:T(8,128)(2,1)} %param.9), kind=kOutput, calls=%fused_computation.1 | convolution fusion | flops 6448742400 | bytes 20971520 | tf_op jit(solution)/shard_map/dot_general | solution.py:36
  145.4 0.0 copy-start.1
  145.4 0.0 copy-start.2
  145.4 0.0 reduce-scatter.2.cloned.1.call-update
  145.5 113.2 %reduce-scatter.2.cloned.1.call-done = bf16[1024,192]{0,1:T(8,128)(2,1)} async-done(((bf16[1024,3072]{0,1:T(8,128)(2,1)}), bf16[1024,192]{0,1:T(8,128)(2,1)}) %reduce-scatter.2.cloned.1.call-update) | async-done | bytes 393232 | tf_op jit(solution)/shard_map/reduce_scatter | solution.py:37
  258.6 2.0 copy.34
  260.6 5.4 %all-to-all-start.1 = ((bf16[16,64,192]{2,1,0:T(8,128)(2,1)}), bf16[16,64,192]{2,1,0:T(8,128)(2,1)}, u32[]{:S(2)}, u32[]{:S(2)}) async-start(bf16[16,64,192]{2,1,0:T(8,128)(2,1)} %bitcast.43), calls=%async_computation.2 | async-start | bytes 1048576 | tf_op jit(solution)/shard_map/all_to_all | solution.py:41
  266.1 0.0 copy-done.1
  266.1 0.1 copy.35
  266.2 0.1 mul.50
  266.4 0.0 copy-done.2
  266.4 0.1 copy.36
  266.6 9.4 %all-to-all-done.1 = bf16[16,64,192]{2,1,0:T(8,128)(2,1)} async-done(((bf16[16,64,192]{2,1,0:T(8,128)(2,1)}), bf16[16,64,192]{2,1,0:T(8,128)(2,1)}, u32[]{:S(2)}, u32[]{:S(2)}) %all-to-all-start.1) | async-done | bytes 393248 | tf_op jit(solution)/shard_map/all_to_all | solution.py:41
  276.0 2.1 bitcast_convert_fusion
  278.1 3.5 %gather_fusion = f32[512,192]{1,0:T(8,128)} fusion(f32[1024,192]{1,0:T(8,128)} %bitcast_convert_fusion, s32[1024]{0:T(1024)S(1)} %pad_clamp_fusion), kind=kCustom, calls=%fused_computation | custom fusion | bytes 788480 | tf_op jit(solution)/shard_map/gather | solution.py:49
  281.5 2.1 gather.6
  283.7 1.8 multiply_reduce_fusion
  285.5 0.7 copy.37
  (9 shorter events, 0.1 us)
Async XLA Ops:
  6.5 126.4 %copy-start = (bf16[1,512,3072]{2,1,0:T(8,128)(2,1)S(1)}, bf16[1,512,3072]{2,1,0:T(8,128)(2,1)}, u32[]{:S(2)}) copy-start(bf16[1,512,3072]{2,1,0:T(8,128)(2,1)} %param.11) | copy-start | bytes 9437188
  6.5 117.9 %all-gather.2.cloned.1.call-start = ((), (), s32[]{:S(2)}) async-start(), calls=%async_computation.3 | async-start | bytes 6684672 | tf_op jit(solution)/shard_map/all_gather | solution.py:32
  33.2 225.4 %reduce-scatter.2.cloned.1.call-start = ((), (), s32[]{:S(2)}) async-start(), calls=%async_computation.4 | async-start | bytes 6684672 | tf_op jit(solution)/shard_map/reduce_scatter | solution.py:37
  145.4 120.6 %copy-start.1 = (s32[256,2]{0,1:T(2,128)S(1)}, s32[256,2]{0,1:T(2,128)}, u32[]{:S(2)}) copy-start(s32[256,2]{0,1:T(2,128)} %param.7) | copy-start | bytes 6148
  145.4 120.9 %copy-start.2 = (f32[256,2]{0,1:T(2,128)S(1)}, f32[256,2]{0,1:T(2,128)}, u32[]{:S(2)}) copy-start(f32[256,2]{0,1:T(2,128)} %param.8) | copy-start | bytes 6148
  260.6 15.3 %all-to-all-start.1 = ((bf16[16,64,192]{2,1,0:T(8,128)(2,1)}), bf16[16,64,192]{2,1,0:T(8,128)(2,1)}, u32[]{:S(2)}, u32[]{:S(2)}) async-start(bf16[16,64,192]{2,1,0:T(8,128)(2,1)} %bitcast.43), calls=%async_computation.2 | async-start | bytes 1048576 | tf_op jit(solution)/shard_map/all_to_all | solution.py:41
Sparse Core Ops, SparseCore 0:
  33.3 91.0 all-gather.1
  145.6 112.9 reduce-scatter.1
where the time goes:
time: 294 us; the launch traced here: 293 us
  waiting for transfers between devices  214 us (73%)
  matrix products  22.6 us (8%)
  blocking collectives  17.2 us (6%)
  local copies, waits for them, and re-layouts  15.3 us (5%)
  between operations  13.5 us (5%)
  starting transfers between devices  5.48 us (2%)
  other arithmetic  5.22 us (2%)
    reduce_scatter x1, waiting for transfers between devices, body(): lax.psum_scatter(terms.astype(jnp.bfloat16), 'split', scatter_dimension=1...  113 us
    all_gather x1, waiting for transfers between devices, body(): piece = lax.all_gather(arrived, 'split', axis=1, tiled=True)  91.2 us
    all_to_all x1, blocking collectives, body(): lax.all_to_all(sending, 'expert', split_axis=0, concat_axis=0, tiled=True)  17.2 us
    dot_general x1, matrix products, body(): terms = jnp.dot(hidden, w_down, preferred_element_type=jnp.float32)  12.5 us
    all_to_all x1, waiting for transfers between devices, body(): lax.all_to_all(result.reshape(experts, capacity, narrow).astype(jnp.bfloa...  9.38 us
    dot_general x1, matrix products, body(): up_part = jnp.dot(piece, w_up, preferred_element_type=jnp.float32)  8.52 us
  transfers between devices with their start and end apart: 3, of which 3 were waited for; matrix products, arithmetic and copies ran while one was open for 0% of the time, Pallas kernels for 0%

commit v1 on v0

v1 whole, which is shorter than its diff:
```python
import functools

import jax
import jax.numpy as jnp
from jax import lax
from jax.experimental import pallas as pl
from jax.experimental.pallas import tpu as pltpu
from jax.sharding import PartitionSpec as P

MESH = pl.DeviceIdType.MESH
BF16 = jnp.bfloat16
F32 = jnp.float32

COLS = 256
GROUPS = 1024 // COLS
PAIRS = COLS // 128
OFFSET = (0, 1, 2, 3, 4, 5, 6, 7, 8)
PARTS = ((0, 160), (160, 32))


def wrap(i, n):
    return lax.rem(i + n, n)


def kernel(
    tok_ref, ids_ref, logit_ref, gate_hbm, up_hbm, down_hbm, out_ref,
    gate_raw, up_raw, down_raw, gate_t, up_t, down_t,
    x_buf, p_buf, hidden, sel, w_high, w_low,
    disp_send, disp_recv, ret_send, ret_recv,
    a1, a2, a3, a4, b1, b2, b3, b4,
    weight_sem, disp_ss, disp_rs, ret_ss, ret_rs, ss, rs,
):
    me = lax.axis_index("expert")
    place = lax.axis_index("split")
    x = me // 4
    z_lo = lax.rem(me // 2, 2)
    z = place // 4
    y = lax.rem(place, 4)
    land = ((a1, a2, a3, a4), (b1, b2, b3, b4))

    def at_z(zz):
        return (me, wrap(zz, 4) * 4 + y)

    def at_y(yy):
        return (me, z * 4 + wrap(yy, 4))

    barrier = pltpu.get_barrier_semaphore()
    for d in range(1, 16):
        pl.semaphore_signal(barrier, inc=1, device_id=(wrap(me + d, 16), place), device_id_type=MESH)
    for dev in (at_z(z + 1), at_z(z - 1), at_y(y + 1), at_y(y - 1)):
        pl.semaphore_signal(barrier, inc=1, device_id=dev, device_id_type=MESH)

    loads = [
        pltpu.make_async_copy(src, dst, weight_sem.at[i])
        for i, (src, dst) in enumerate(((gate_hbm, gate_raw), (up_hbm, up_raw), (down_hbm, down_raw)))
    ]
    for c in loads:
        c.start()

    ids = ids_ref[...]
    labels = lax.broadcasted_iota(jnp.int32, (16, 256), 0)
    hit0 = ids[0:1, :] == labels
    hit1 = ids[1:2, :] == labels
    hits = jnp.where(hit0 | hit1, 1.0, 0.0).astype(F32)
    earlier = lax.broadcasted_iota(jnp.int32, (256, 256), 0) < lax.broadcasted_iota(jnp.int32, (256, 256), 1)
    count = jnp.dot(hits.astype(BF16), jnp.where(earlier, 1.0, 0.0).astype(BF16), preferred_element_type=F32)
    slot = jnp.where(hits > 0.5, count, -1.0).astype(jnp.int32)
    logits = logit_ref[...]
    first = 1.0 / (1.0 + jnp.exp(logits[1:2, :] - logits[0:1, :]))
    weight = jnp.where(hit0, first, jnp.where(hit1, 1.0 - first, 0.0))
    sub = lax.broadcasted_iota(jnp.int32, (64, 256), 0)
    zero = jnp.zeros((64, 256), BF16)
    for e in range(16):
        low, mid, high = e * 128, e * 128 + 64, e * 128 + 128
        one = jnp.where(sub == slot[e:e + 1, :], 1.0, 0.0).astype(BF16)
        sel[low:mid, 0:256] = one
        sel[low:mid, 256:512] = zero
        sel[mid:high, 0:256] = zero
        sel[mid:high, 256:512] = one

    tok = tok_ref[...]
    halves = jnp.concatenate([tok[0:96, :], tok[96:192, :]], axis=1)
    for e in range(16):
        disp_send[e] = lax.dot_general(
            halves, sel[e * 128:e * 128 + 128, :], (((1,), (1,)), ((), ())), preferred_element_type=F32
        ).astype(BF16)
    disp_recv[pl.ds(me, 1)] = disp_send[pl.ds(me, 1)]

    def dispatch(d):
        step, inner = d // 4, d % 4
        far = (0, 1, 3, 2)[step]
        target = wrap(x + far, 4) * 4 + wrap(me - x * 4 + inner, 4)
        return pltpu.make_async_remote_copy(
            src_ref=disp_send.at[target], dst_ref=disp_recv.at[me], send_sem=disp_ss.at[d],
            recv_sem=disp_rs.at[me], device_id=(target, place), device_id_type=MESH)

    pl.semaphore_wait(barrier, 19)
    for d in range(1, 16):
        dispatch(d).start()

    for e in range(16):
        low, mid, high = e * 128, e * 128 + 64, e * 128 + 128
        w = weight[e:e + 1, :]
        full = jnp.where(sub == slot[e:e + 1, :], w, 0.0)
        top = full.astype(BF16)
        rest = (full - top.astype(F32)).astype(BF16)
        for ref, val in ((w_high, top), (w_low, rest)):
            ref[low:mid, 0:256] = val
            ref[low:mid, 256:512] = zero
            ref[mid:high, 0:256] = zero
            ref[mid:high, 256:512] = val

    def pick(ref, g, part, i, j, r0, rows):
        zi, yi = (i, j) if part == 0 else (j, i)
        return ref.at[g, zi, yi, pl.ds(r0, rows), :]

    def coords(part):
        return (z, y) if part == 0 else (y, z)

    def device(part, axis, i):
        return at_z(i) if (axis == 0) == (part == 0) else at_y(i)

    def gather_refs(part, step, sign, g, arriving):
        u, v = coords(part)
        r0, rows = PARTS[part]
        half = rows // 2
        du, dv = (-sign, -sign) if arriving else (0, 0)
        lo = sign > 0
        if step == 0:
            return pick(x_buf, g, part, wrap(u + du, 4), v, r0, rows)
        if step == 1:
            return pick(x_buf, g, part, wrap(u - sign + du + 4, 4), v, r0 if lo else r0 + half, half)
        if step == 2:
            return pick(x_buf, g, part, slice(0, 4), wrap(v + dv, 4), r0, rows)
        return pick(x_buf, g, part, slice(0, 2) if lo else slice(2, 4), wrap(v - sign + dv + 4, 4), r0, rows)

    def gather(part, step, sign, g):
        u, v = coords(part)
        ref = gather_refs(part, step, sign, g, False)
        axis = 0 if step < 2 else 1
        k = step * 2 + (0 if sign > 0 else 1)
        return pltpu.make_async_remote_copy(
            src_ref=ref, dst_ref=ref, send_sem=ss.at[g, part, k], recv_sem=rs.at[g, part, k],
            device_id=device(part, axis, (u if axis == 0 else v) + sign), device_id_type=MESH)

    def gather_wait(part, step, sign, g):
        u, v = coords(part)
        ref = gather_refs(part, step, sign, g, True)
        axis = 0 if step < 2 else 1
        k = step * 2 + (0 if sign > 0 else 1)
        pltpu.make_async_remote_copy(
            src_ref=ref, dst_ref=ref, send_sem=ss.at[g, part, k], recv_sem=rs.at[g, part, k],
            device_id=device(part, axis, (u if axis == 0 else v) + sign), device_id_type=MESH).wait_recv()

    def scatter(part, step, sign, g):
        u, v = coords(part)
        r0, rows = PARTS[part]
        half = rows // 2
        lo = sign > 0
        side = 0 if lo else 1
        if step == 0:
            src = pick(p_buf, g, part, slice(0, 2) if lo else slice(2, 4), wrap(v + 2, 4), r0, rows)
        elif step == 1:
            src = pick(p_buf, g, part, slice(0, 4), wrap(v + sign, 4), r0, rows)
        elif step == 2:
            src = pick(p_buf, g, part, wrap(u + 2, 4), v, r0 if lo else r0 + half, half)
        else:
            src = pick(p_buf, g, part, wrap(u + sign, 4), v, r0, rows)
        axis = 1 if step < 2 else 0
        k = 8 + step * 2 + side
        return pltpu.make_async_remote_copy(
            src_ref=src, dst_ref=land[part][step].at[g, side], send_sem=ss.at[g, part, k], recv_sem=rs.at[g, part, k],
            device_id=device(part, axis, (u if axis == 0 else v) + sign), device_id_type=MESH)

    def add_into(ref, *others):
        total = ref[...].astype(F32)
        for o in others:
            total = total + o[...].astype(F32)
        ref[...] = total.astype(BF16)

    BOTH = ((0, 1), (0, -1), (1, 1), (1, -1))

    def blocks_of(g, i):
        q = g * PAIRS + i
        h = q // 2
        far = h + (h // 2) * (1 - 2 * lax.rem(h, 2))
        return lax.rem(x + far, 4) * 4 + lax.rem(z_lo + lax.rem(q, 2), 2) * 2

    def arrive(g):
        for i in range(PAIRS):
            b0 = blocks_of(g, i)
            for b in (b0, b0 + 1):
                @pl.when(b != me)
                def _():
                    pltpu.make_async_remote_copy(
                        src_ref=disp_send.at[b], dst_ref=disp_recv.at[b], send_sem=disp_ss.at[0],
                        recv_sem=disp_rs.at[b], device_id=(b, place), device_id_type=MESH).wait_recv()
            one, two = disp_recv[b0], disp_recv[b0 + 1]
            x_buf[g, z, y, 0:96, i * 128:i * 128 + 128] = jnp.concatenate([one[:, :64], two[:, :64]], axis=1)
            x_buf[g, z, y, 96:192, i * 128:i * 128 + 128] = jnp.concatenate([one[:, 64:], two[:, 64:]], axis=1)

    def multiply(g):
        rows = x_buf[g].reshape(3072, COLS)

        @pl.loop(0, 2)
        def _(i):
            m = pl.ds(pl.multiple_of(i * 256, 256), 256)
            gate = jnp.dot(gate_t[m, :], rows, preferred_element_type=F32)
            up = jnp.dot(up_t[m, :], rows, preferred_element_type=F32)
            hidden[m, :] = (gate / (1.0 + jnp.exp(-gate)) * up).astype(BF16)

        @pl.loop(0, 4)
        def _(i):
            m = pl.ds(pl.multiple_of(i * 768, 768), 768)
            part = jnp.dot(down_t[m, :], hidden[...], preferred_element_type=F32)
            p_buf[g, i] = part.astype(BF16).reshape(4, 192, COLS)

    def give_back(g):
        rows = []
        for part in (0, 1):
            u, v = coords(part)
            r0, n = PARTS[part]
            total = pick(p_buf, g, part, u, v, r0, n)[...].astype(F32)
            total = total + land[part][3][g, 0].astype(F32) + land[part][3][g, 1].astype(F32)
            rows.append(total.astype(BF16))
        whole = jnp.concatenate(rows, axis=0)
        for i in range(PAIRS):
            b0 = blocks_of(g, i)
            tile = whole[:, i * 128:i * 128 + 128]
            for k in (0, 1):
                lanes = slice(k * 64, k * 64 + 64)
                ret_send[g, i, k] = jnp.concatenate([tile[0:96, lanes], tile[96:192, lanes]], axis=1)

                @pl.when(b0 + k != me)
                def _():
                    returning(g, i, k).start()

                @pl.when(b0 + k == me)
                def _():
                    ret_recv[pl.ds(me, 1)] = ret_send[g, i, pl.ds(k, 1)]

    def returning(g, i, k):
        target = blocks_of(g, i) + k
        return pltpu.make_async_remote_copy(
            src_ref=ret_send.at[g, i, k], dst_ref=ret_recv.at[me], send_sem=ret_ss.at[g, i, k],
            recv_sem=ret_rs.at[me], device_id=(target, place), device_id_type=MESH)

    def stage(k, g):
        if k == 0:
            arrive(g)
            for part, sign in BOTH:
                gather(part, 0, sign, g).start()
        elif k < 4:
            for part, sign in BOTH:
                gather_wait(part, k - 1, sign, g)
            for part, sign in BOTH:
                gather(part, k, sign, g).start()
        elif k == 4:
            for part, sign in BOTH:
                gather_wait(part, 3, sign, g)
            multiply(g)
            for part, sign in BOTH:
                scatter(part, 0, sign, g).start()
        else:
            step = k - 5
            for part, sign in BOTH:
                scatter(part, step, sign, g).wait_recv()
            if k == 8:
                give_back(g)
                return
            for part in (0, 1):
                u, v = coords(part)
                r0, n = PARTS[part]
                half = n // 2
                got = land[part][step]
                if step == 0:
                    add_into(pick(p_buf, g, part, slice(0, 2), wrap(v + 1, 4), r0, n), got.at[g, 0])
                    add_into(pick(p_buf, g, part, slice(2, 4), wrap(v - 1, 4), r0, n), got.at[g, 1])
                elif step == 1:
                    add_into(pick(p_buf, g, part, slice(0, 4), v, r0, n), got.at[g, 0], got.at[g, 1])
                else:
                    add_into(pick(p_buf, g, part, wrap(u + 1, 4), v, r0, half), got.at[g, 0])
                    add_into(pick(p_buf, g, part, wrap(u - 1, 4), v, r0 + half, half), got.at[g, 1])
                for sign in (1, -1):
                    scatter(part, step + 1, sign, g).start()

    def tick(t):
        for k in range(8, -1, -1):
            g = t - OFFSET[k]

            @pl.when((g >= 0) & (g < GROUPS))
            def _():
                stage(k, g)

    def prepare():
        for c in loads:
            c.wait()

        @pl.loop(0, 12)
        def _(i):
            m = pl.ds(pl.multiple_of(i * 256, 256), 256)
            gate_t[:, m] = gate_raw[m, :].T
            up_t[:, m] = up_raw[m, :].T
            down_t[m, :] = down_raw[:, m].T

    pl.loop(0, 2)(tick)
    prepare()
    pl.loop(2, OFFSET[8] + GROUPS)(tick)

    for d in range(1, 16):
        src = wrap(me + d, 16)
        pltpu.make_async_remote_copy(
            src_ref=disp_send.at[src], dst_ref=ret_recv.at[src], send_sem=disp_ss.at[0],
            recv_sem=ret_rs.at[src], device_id=(src, place), device_id_type=MESH).wait_recv()
    back = jnp.concatenate([ret_recv[e] for e in range(16)], axis=1)
    mixed = jnp.dot(back, w_high[...], preferred_element_type=F32) + jnp.dot(
        back, w_low[...], preferred_element_type=F32)
    out_ref[0:96, :] = mixed[:, 0:256].astype(BF16)
    out_ref[96:192, :] = mixed[:, 256:512].astype(BF16)

    for d in range(1, 16):
        dispatch(d).wait_send()

    @pl.loop(0, GROUPS)
    def _(g):
        for part, sign in BOTH:
            for step in range(4):
                gather(part, step, sign, g).wait_send()
                scatter(part, step, sign, g).wait_send()
        for i in range(PAIRS):
            for k in (0, 1):
                @pl.when(blocks_of(g, i) + k != me)
                def _():
                    returning(g, i, k).wait_send()


def body(tokens, expert_ids, pair_logits, gate_weight, up_weight, down_weight):
    vmem = pl.BlockSpec(memory_space=pltpu.VMEM)
    hbm = pl.BlockSpec(memory_space=pl.ANY)
    dma = pltpu.SemaphoreType.DMA
    landing = []
    for part in (0, 1):
        n = PARTS[part][1]
        landing += [
            pltpu.VMEM((GROUPS, 2, 2, n, COLS), BF16),
            pltpu.VMEM((GROUPS, 2, 4, n, COLS), BF16),
            pltpu.VMEM((GROUPS, 2, n // 2, COLS), BF16),
            pltpu.VMEM((GROUPS, 2, n, COLS), BF16),
        ]
    out = pl.pallas_call(
        kernel,
        out_shape=jax.ShapeDtypeStruct((192, 256), BF16),
        in_specs=[vmem, vmem, vmem, hbm, hbm, hbm],
        out_specs=vmem,
        scratch_shapes=[
            pltpu.VMEM((3072, 512), BF16), pltpu.VMEM((3072, 512), BF16), pltpu.VMEM((512, 3072), BF16),
            pltpu.VMEM((512, 3072), BF16), pltpu.VMEM((512, 3072), BF16), pltpu.VMEM((3072, 512), BF16),
            pltpu.VMEM((GROUPS, 4, 4, 192, COLS), BF16), pltpu.VMEM((GROUPS, 4, 4, 192, COLS), BF16),
            pltpu.VMEM((512, COLS), BF16),
            pltpu.VMEM((2048, 512), BF16), pltpu.VMEM((2048, 512), BF16), pltpu.VMEM((2048, 512), BF16),
            pltpu.VMEM((16, 96, 128), BF16), pltpu.VMEM((16, 96, 128), BF16),
            pltpu.VMEM((GROUPS, PAIRS, 2, 96, 128), BF16), pltpu.VMEM((16, 96, 128), BF16),
            *landing,
            dma((3,)), dma((16,)), dma((16,)), dma((GROUPS, PAIRS, 2)), dma((16,)),
            dma((GROUPS, 2, 16)), dma((GROUPS, 2, 16)),
        ],
        compiler_params=pltpu.CompilerParams(
            collective_id=0, has_side_effects=True, vmem_limit_bytes=60 * 2**20),
        cost_estimate=pl.CostEstimate(flops=9_700_000_000, bytes_accessed=10_000_000, transcendentals=524288),
    )(tokens.T, expert_ids.T, pair_logits.T, gate_weight[0], up_weight[0], down_weight[0])
    return out.T


def solution(mesh):
    in_specs = (
        P("expert", "split"),
        P("expert", None),
        P("expert", None),
        P("expert", None, "split"),
        P("expert", None, "split"),
        P("expert", "split", None),
    )
    return jax.shard_map(body, mesh=mesh, in_specs=in_specs, out_specs=P("expert", "split"), check_vma=False)
```

time: 294 us -> 137 us (0.47)
  waiting for transfers between devices: 214 us -> 0 us
  Pallas kernels: 0 us -> 135 us
  matrix products: 22.6 us -> 0 us
  blocking collectives: 17.2 us -> 0 us
  local copies, waits for them, and re-layouts: 15.3 us -> 1.54 us
  between operations: 13.5 us -> 0.01 us
  starting transfers between devices: 5.48 us -> 0 us
  other arithmetic: 5.22 us -> 0 us
    pallas_call x0 -> x1, Pallas kernels: none -> 135 us  [body(): pl.pallas_call(kernel, out_shape=jax.ShapeDtypeStruct((192, 256), BF16),...]
    reduce_scatter x1 -> x0, waiting for transfers between devices: 113 us -> none  [body(): lax.psum_scatter(terms.astype(jnp.bfloat16), 'split', scatter_dimension=1...]
    all_gather x1 -> x0, waiting for transfers between devices: 91.2 us -> none  [body(): piece = lax.all_gather(arrived, 'split', axis=1, tiled=True)]
    dot_general x3 -> x0, matrix products: 22.6 us -> none  [the longest x1 12.5 us: body(): terms = jnp.dot(hidden, w_down, preferred_element_type=jnp.float32)]
    all_to_all x1 -> x0, blocking collectives: 17.2 us -> none  [body(): lax.all_to_all(sending, 'expert', split_axis=0, concat_axis=0, tiled=True)]
    all_to_all x1 -> x0, waiting for transfers between devices: 9.38 us -> none  [body(): lax.all_to_all(result.reshape(experts, capacity, narrow).astype(jnp.bfloa...]
    gather x2 -> x0, local copies, waits for them, and re-layouts: 5.6 us -> none  [body(): picked = returned[dest] * mix[:, None]]
    all_to_all x1 -> x0, starting transfers between devices: 5.43 us -> none  [body(): lax.all_to_all(result.reshape(experts, capacity, narrow).astype(jnp.bfloa...]
  transfers between devices with their start and end apart: 3 -> 0, of which waited for: 3 -> 0; matrix products, arithmetic and copies ran while one was open for 0% -> 0% of each run, Pallas kernels for 0% -> 0%
where the time goes in v1:
time: 137 us; the launch traced here: 136 us
  Pallas kernels  135 us (99%)
  local copies, waits for them, and re-layouts  1.54 us (1%)
    pallas_call x1, Pallas kernels, body(): pl.pallas_call(kernel, out_shape=jax.ShapeDtypeStruct((192, 256), BF16),...  135 us

profile of v1, /device:TPU:1, one launch (start us, length us, event | category | flops | bytes accessed | tf_op | source)
XLA Modules:
  0.0 136.4 jit_solution(4736270173901783815)
XLA Ops:
  0.0 134.8 %shard_map.64 = bf16[192,256]{1,0:T(8,128)(2,1)} custom-call(bf16[192,256]{1,0:T(8,128)(2,1)} %bitcast.11, s32[2,256]{1,0:T(2,128)} %bitcast.12, f32[2,256]{1,0:T(2,128)} %bitcast.13, bf16[3072,512]{1,0:T(8,128)(2,1)} %bitcast.8, bf16[3072,512]{1,0:T(8,128)(2,1)} %bitcast.9, bf16[512,3072]{1,0:T(8,128)(2,1)} %bitcast.10), custom_call_target="tpu_custom_call" | custom-call | flops 9699999744 | bytes 10000000 | tf_op jit(solution)/shard_map/pallas_call | solution.py:350
  134.8 1.5 %copy.8 = bf16[256,192]{0,1:T(8,128)(2,1)} copy(bf16[256,192]{0,1:T(8,128)(2,1)} %bitcast.7) | data formatting | bytes 196608

commit v2 on v0

v2 whole, which is shorter than its diff:
```python
import functools

import jax
import jax.numpy as jnp
from jax import lax
from jax.experimental import pallas as pl
from jax.experimental.pallas import tpu as pltpu
from jax.sharding import PartitionSpec as P

MESH = pl.DeviceIdType.MESH
BF16 = jnp.bfloat16
F32 = jnp.float32

COLS = 256
GROUPS = 4
PARTS = ((0, 128),)
RA = 128
RC = 64
HA, HC = RA // 2, RC // 2
ORDER = (
    ("g", 0, 0, 0), ("h", 1), ("h", 2), ("g", 1, 0, 0), ("g", 0, 1, 0), ("g", 2, 0, 0),
    ("h", 3), ("prep", 3), ("prep", 0), ("prep", 1), ("tab",), ("g", 1, 1, 0),
    ("h", 4), ("g", 2, 1, 0), ("g", 0, 3, 0), ("h", 5), ("g", 3, 0, 0), ("g", 1, 3, 0),
    ("pk", 1), ("g", 3, 1, 0), ("pk", 3), ("g", 2, 3, 0), ("prep", 2), ("g", 0, 2, 0),
    ("pk", 0), ("mu", 0), ("mc", 0), ("ma", 0), ("g", 1, 2, 0), ("pk", 2),
    ("g", 2, 2, 0), ("add", 0), ("g", 3, 3, 0), ("mu", 1), ("mc", 1), ("ma", 1),
    ("mu", 3), ("g", 3, 2, 0), ("mc", 3), ("s", 1, 0, 0), ("ma", 3), ("mu", 2),
    ("s", 1, 1, 0), ("mc", 2), ("s", 2, 0, 0), ("s", 3, 0, 0), ("s", 1, 3, 0), ("ma", 2),
    ("s", 2, 1, 0), ("s", 4, 0, 0), ("s", 3, 1, 0), ("add", 1), ("add", 3), ("add", 2),
    ("t", 0), ("s", 2, 3, 0), ("t", 1), ("s", 1, 2, 0), ("s", 3, 3, 0), ("s", 4, 1, 0),
    ("t", 2), ("s", 4, 3, 0), ("s", 2, 2, 0), ("t", 3), ("s", 3, 2, 0), ("own",),
    ("t", 4), ("s", 4, 2, 0), ("t", 5),
)
FAR = (0, 1, 3, 2)


def wrap(i, n):
    return lax.rem(i + n, n)


def kernel(
    tok_ref, ids_ref, logit_ref, gate_hbm, up_hbm, down_hbm, out_ref,
    gate_raw, up_raw, down_raw, gate_t, up_t, down_t,
    xa, pa, hidden, sel, w_high, w_low,
    disp_send, disp_recv, ret_send, ret_recv, a1, a2, a3, a4,
    meta, slots, mixes, sel_c, wc_high, wc_low,
    raw, xs, xc, pc, tr, acc, tsum, z1, z2, z3, z4, y1, y2,
    weight_sem, disp_ss, disp_rs, ret_ss, ret_rs, ss, rs, cs, cr, xss, xrs, tss, trs, local_sem,
):
    me = lax.axis_index("expert")
    place = lax.axis_index("split")
    x = me // 4
    zl = lax.rem(me // 2, 2)
    c = lax.rem(me, 2)
    z = place // 4
    y = lax.rem(place, 4)
    z8 = z * 2 + zl

    def at_z(zz):
        return (me, wrap(zz, 4) * 4 + y)

    def at_y(yy):
        return (me, z * 4 + wrap(yy, 4))

    def at_z8(zz):
        w = wrap(zz, 8)
        return (x * 4 + lax.rem(w, 2) * 2 + c, (w // 2) * 4 + y)

    def at_x(r, core):
        return (lax.rem(x + r, 4) * 4 + zl * 2 + core, place)

    def remote(src, dst, send, recv, dev):
        return pltpu.make_async_remote_copy(
            src_ref=src, dst_ref=dst, send_sem=send, recv_sem=recv, device_id=dev, device_id_type=MESH)

    barrier = pltpu.get_barrier_semaphore()
    for d in range(1, 16):
        pl.semaphore_signal(barrier, inc=1, device_id=(wrap(me + d, 16), place), device_id_type=MESH)
    for dev in (at_z(z + 1), at_z(z - 1), at_y(y + 1), at_y(y - 1), at_z8(z8 + 2 * zl - 1)):
        pl.semaphore_signal(barrier, inc=1, device_id=dev, device_id_type=MESH)

    loads = [
        pltpu.make_async_copy(src, dst, weight_sem.at[i])
        for i, (src, dst) in enumerate(((gate_hbm, gate_raw), (up_hbm, up_raw), (down_hbm, down_raw)))
    ]
    for load in loads:
        load.start()

    tok = tok_ref[...]
    raw[z8, y] = tok[RA:, :]
    meta[zl, 0:2, :] = ids_ref[...].astype(F32)
    meta[zl, 2:4, :] = logit_ref[...]
    meta[zl, 4:8, :] = jnp.zeros((4, 256), F32)

    def swap_meta():
        return remote(meta.at[zl], meta.at[zl], cs.at[24], cr.at[24], (x * 4 + (1 - zl) * 2 + c, place))

    def head(step, sign, arriving=False):
        lo = sign > 0
        k = step * 2 + (0 if lo else 1)
        back = -sign if arriving else 0
        if step == 0:
            ref = raw.at[z8, wrap(y + back, 4)]
        elif step == 1:
            ref = raw.at[z8, wrap(y - sign + back + 4, 4), pl.ds(0 if lo else HC, HC)]
        else:
            n = step - 2
            chunk = wrap(z8 - sign * n + back + 8, 8)
            ref = raw.at[chunk] if n < 3 else raw.at[chunk, pl.ds(0 if lo else 2, 2)]
        return remote(ref, ref, cs.at[k], cr.at[k], at_y(y + sign) if step < 2 else at_z8(z8 + sign))

    def head_step(step):
        for sign in (1, -1):
            head(step - 1, sign, True).wait_recv()
        for sign in (1, -1):
            head(step, sign).start()

    labels = lax.broadcasted_iota(jnp.int32, (16, 256), 0).astype(F32)
    earlier = lax.broadcasted_iota(jnp.int32, (256, 256), 0) < lax.broadcasted_iota(jnp.int32, (256, 256), 1)
    earlier = jnp.where(earlier, 1.0, 0.0).astype(BF16)
    sub = lax.broadcasted_iota(jnp.int32, (64, 256), 0).astype(F32)
    zero = jnp.zeros((64, 256), BF16)

    def slot_of(ids):
        hits = jnp.where((ids[0:1, :] == labels) | (ids[1:2, :] == labels), 1.0, 0.0)
        count = jnp.dot(hits.astype(BF16), earlier, preferred_element_type=F32)
        return jnp.where(hits > 0.5, count, -1.0)

    def mix_of(ids, logits):
        first = 1.0 / (1.0 + jnp.exp(logits[1:2, :] - logits[0:1, :]))
        return jnp.where(ids[0:1, :] == labels, first, jnp.where(ids[1:2, :] == labels, 1.0 - first, 0.0))

    ids = ids_ref[...].astype(F32)
    slot = slot_of(ids)
    mix = mix_of(ids, logit_ref[...])

    def one_hot(row):
        return jnp.where(sub == row, 1.0, 0.0).astype(BF16)

    def split(row, w):
        full = jnp.where(sub == row, w, 0.0)
        top = full.astype(BF16)
        return top, (full - top.astype(F32)).astype(BF16)

    def place_two(ref, base, first, second):
        ref[base:base + 64, 0:256] = first
        ref[base:base + 64, 256:512] = zero
        ref[base + 64:base + 128, 0:256] = zero
        ref[base + 64:base + 128, 256:512] = second

    for e in range(16):
        one = one_hot(slot[e:e + 1, :])
        place_two(sel, e * 128, one, one)

    halves = jnp.concatenate([tok[0:HA, :], tok[HA:RA, :]], axis=1)
    for e in range(16):
        disp_send[e] = lax.dot_general(
            halves, sel[e * 128:e * 128 + 128, :], (((1,), (1,)), ((), ())), preferred_element_type=F32
        ).astype(BF16)
    disp_recv[pl.ds(me, 1)] = disp_send[pl.ds(me, 1)]

    def dispatch(d):
        step, inner = d // 4, d % 4
        target = wrap(x + FAR[step], 4) * 4 + wrap(me - x * 4 + inner, 4)
        return remote(disp_send.at[target], disp_recv.at[me], disp_ss.at[d], disp_rs.at[me], (target, place))

    pl.semaphore_wait(barrier, 20)
    swap_meta().start()
    for sign in (1, -1):
        head(0, sign).start()
    for d in range(1, 16):
        dispatch(d).start()

    def tables():
        remote(meta.at[zl], meta.at[1 - zl], cs.at[24], cr.at[24], (x * 4 + (1 - zl) * 2 + c, place)).wait_recv()
        for b in (0, 1):
            both = meta[b]
            slots[b] = slot_of(both[0:2])
            mixes[b] = mix_of(both[0:2], both[2:4])
        for r in range(4):
            for core in (0, 1):
                e = lax.rem(x + r, 4) * 4 + zl * 2 + core
                base = r * 256 + core * 128
                row = [slots[b, pl.ds(e, 1), :] for b in (0, 1)]
                w = [mixes[b, pl.ds(e, 1), :] for b in (0, 1)]
                place_two(sel_c, base, one_hot(row[0]), one_hot(row[1]))
                first, second = split(row[0], w[0]), split(row[1], w[1])
                place_two(wc_high, base, first[0], second[0])
                place_two(wc_low, base, first[1], second[1])

    def own_weights():
        for e in range(16):
            top, rest = split(slot[e:e + 1, :], mix[e:e + 1, :])
            place_two(w_high, e * 128, top, top)
            place_two(w_low, e * 128, rest, rest)

    def x_out(r, core):
        return remote(xs.at[r, core], xc.at[(4 - r) % 4, c], xss.at[r, core], xrs.at[(4 - r) % 4, c], at_x(r, core))

    def x_back(r, core):
        return remote(pc.at[r, core], tr.at[(4 - r) % 4, c], tss.at[r, core], trs.at[(4 - r) % 4, c], at_x(r, core))

    def keep(out):
        src, dst, i = (xs.at[0, c], xc.at[0, c], 0) if out else (pc.at[0, c], tr.at[0, c], 1)
        return pltpu.make_async_copy(src, dst, local_sem.at[i])

    def x_arrived(refs, sems, r, core):
        remote(refs.at[r, core], refs.at[r, core], xss.at[0, 0], sems.at[r, core], at_x(r, core)).wait_recv()

    def pick_slots(r):
        base = r * 256

        @pl.loop(0, 4)
        def _(i):
            first = raw[i * 2].reshape(4 * RC, 256)
            second = raw[i * 2 + 1].reshape(4 * RC, 256)
            got = lax.dot_general(
                first, sel_c[base:base + 256, 0:256], (((1,), (1,)), ((), ())), preferred_element_type=F32)
            got = got + lax.dot_general(
                second, sel_c[base:base + 256, 256:512], (((1,), (1,)), ((), ())), preferred_element_type=F32)
            got = got.astype(BF16)
            s = pl.ds(i * 4, 4)
            xs[r, 0, s] = got[:, :128].reshape(4, RC, 128)
            xs[r, 1, s] = got[:, 128:].reshape(4, RC, 128)

        if r == 0:
            keep(True).start()
            x_out(0, 1 - c).start()
        else:
            for core in (0, 1):
                x_out(r, core).start()

    def wait_slots(r):
        if r == 0:
            keep(True).wait()
            x_arrived(xc, xrs, 0, 1 - c)
        else:
            for core in (0, 1):
                x_arrived(xc, xrs, r, core)

    def add_up(r, first, last):
        if r == 0:
            keep(False).wait()
            x_arrived(tr, trs, 0, 1 - c)
        else:
            for core in (0, 1):
                x_arrived(tr, trs, r, core)

        @pl.loop(0, 4)
        def _(i):
            s = pl.ds(i * 4, 4)
            rows = jnp.concatenate(
                [tr[r, 0, s].reshape(4 * RC, 128), tr[r, 1, s].reshape(4 * RC, 128)], axis=1)
            base = r * 256
            total = jnp.dot(rows, wc_high[base:base + 256, :], preferred_element_type=F32)
            total = total + jnp.dot(rows, wc_low[base:base + 256, :], preferred_element_type=F32)
            if not first:
                total = total + acc[i]
            if last:
                total = total.astype(BF16)
                tsum[i * 2] = total[:, 0:256].reshape(4, RC, 256)
                tsum[i * 2 + 1] = total[:, 256:512].reshape(4, RC, 256)
            else:
                acc[i] = total

    def add_into(ref, *others):
        total = ref[...].astype(F32)
        for o in others:
            total = total + o[...].astype(F32)
        ref[...] = total.astype(BF16)

    tail_land = (z1, z2, z3, z4, y1, y2)

    def tail(step, sign):
        lo = sign > 0
        side = 0 if lo else 1
        k = 12 + step * 2 + side
        if step == 0:
            src = tsum.at[wrap(z8 + 4, 8), pl.ds(0 if lo else 2, 2)]
        elif step < 4:
            src = tsum.at[wrap(z8 + sign * (4 - step), 8)]
        elif step == 4:
            src = tsum.at[z8, wrap(y + 2, 4), pl.ds(0 if lo else HC, HC)]
        else:
            src = tsum.at[z8, wrap(y + sign, 4)]
        return remote(src, tail_land[step].at[side], cs.at[k], cr.at[k],
                      at_z8(z8 + sign) if step < 4 else at_y(y + sign))

    def tail_step(step):
        if step > 0:
            for sign in (1, -1):
                tail(step - 1, sign).wait_recv()
        got = tail_land[step - 1]
        if step == 1:
            add_into(tsum.at[wrap(z8 + 3, 8), pl.ds(0, 2)], got.at[0])
            add_into(tsum.at[wrap(z8 - 3, 8), pl.ds(2, 2)], got.at[1])
        elif step in (2, 3):
            add_into(tsum.at[wrap(z8 + 4 - step, 8)], got.at[0])
            add_into(tsum.at[wrap(z8 - 4 + step, 8)], got.at[1])
        elif step == 4:
            add_into(tsum.at[z8], got.at[0], got.at[1])
        elif step == 5:
            add_into(tsum.at[z8, wrap(y + 1, 4), pl.ds(0, HC)], got.at[0])
            add_into(tsum.at[z8, wrap(y - 1, 4), pl.ds(HC, HC)], got.at[1])
        for sign in (1, -1):
            tail(step, sign).start()

    land = ((a1, a2, a3, a4),)

    def at_part(ref, r, part, i, j, half=None):
        r0, n = PARTS[part]
        zi, yi = (i, j) if part == 0 else (j, i)
        if half is None:
            return ref.at[r, zi, yi, pl.ds(r0, n)]
        if n % 32 == 0:
            return ref.at[r, zi, yi, pl.ds(r0 + half * (n // 2), n // 2)]
        return ref.at[r, zi, yi, pl.ds(r0, n), pl.ds(half * 128, 128)]

    def coords(part):
        return (z, y) if part == 0 else (y, z)

    def device(part, axis, i):
        return at_z(i) if axis == part else at_y(i)

    ALL, LOW, HIGH = pl.ds(0, 4), pl.ds(0, 2), pl.ds(2, 2)

    def gather(part, step, sign, r, arriving=False):
        u, v = coords(part)
        back = -sign if arriving else 0
        lo = sign > 0
        if step == 0:
            ref = at_part(xa, r, part, wrap(u + back, 4), v)
        elif step == 1:
            ref = at_part(xa, r, part, wrap(u - sign + back + 4, 4), v, 0 if lo else 1)
        elif step == 2:
            ref = at_part(xa, r, part, ALL, wrap(v + back, 4))
        else:
            ref = at_part(xa, r, part, LOW if lo else HIGH, wrap(v - sign + back + 4, 4))
        k = step * 2 + (0 if lo else 1)
        axis = 0 if step < 2 else 1
        return remote(ref, ref, ss.at[r, part, k], rs.at[r, part, k],
                      device(part, axis, (u if axis == 0 else v) + sign))

    def scatter(part, step, sign, r):
        u, v = coords(part)
        lo = sign > 0
        side = 0 if lo else 1
        if step == 0:
            src = at_part(pa, r, part, LOW if lo else HIGH, wrap(v + 2, 4))
        elif step == 1:
            src = at_part(pa, r, part, ALL, wrap(v + sign, 4))
        elif step == 2:
            src = at_part(pa, r, part, wrap(u + 2, 4), v, side)
        else:
            src = at_part(pa, r, part, wrap(u + sign, 4), v)
        k = 8 + step * 2 + side
        axis = 1 if step < 2 else 0
        return remote(src, land[part][step].at[r, side], ss.at[r, part, k], rs.at[r, part, k],
                      device(part, axis, (u if axis == 0 else v) + sign))

    def block_of(r, core, b):
        return lax.rem(x + r, 4) * 4 + b * 2 + core

    def arrive(r):
        for core in (0, 1):
            for b in (0, 1):
                src = block_of(r, core, b)

                @pl.when(src != me)
                def _():
                    remote(disp_recv.at[src], disp_recv.at[src], disp_ss.at[0], disp_rs.at[src],
                           (src, place)).wait_recv()
            one, two = disp_recv[block_of(r, core, 0)], disp_recv[block_of(r, core, 1)]
            lanes = slice(core * 128, core * 128 + 128)
            xa[r, z, y, 0:HA, lanes] = jnp.concatenate([one[:, :64], two[:, :64]], axis=1)
            xa[r, z, y, HA:RA, lanes] = jnp.concatenate([one[:, 64:], two[:, 64:]], axis=1)

    def units(r):
        for part in range(len(PARTS)):
            for sign in (1, -1):
                gather(part, 3, sign, r, True).wait_recv()
        wait_slots(r)
        rows = xa[r].reshape(16 * RA, COLS)
        more = jnp.concatenate([xc[r, 0].reshape(16 * RC, 128), xc[r, 1].reshape(16 * RC, 128)], axis=1)

        @pl.loop(0, 2)
        def _(i):
            m = pl.ds(pl.multiple_of(i * 256, 256), 256)

            def product(w):
                return jnp.dot(w[m, 0:16 * RA], rows, preferred_element_type=F32) + jnp.dot(
                    w[m, 16 * RA:], more, preferred_element_type=F32)

            gate, up = product(gate_t), product(up_t)
            hidden[m, :] = (gate / (1.0 + jnp.exp(-gate)) * up).astype(BF16)

    def results_c(r):
        @pl.loop(0, 2)
        def _(i):
            m = pl.ds(pl.multiple_of(16 * RA + i * 8 * RC, 128), 8 * RC)
            part = jnp.dot(down_t[m, :], hidden[...], preferred_element_type=F32).astype(BF16)
            s = pl.ds(i * 8, 8)
            pc[r, 0, s] = part[:, :128].reshape(8, RC, 128)
            pc[r, 1, s] = part[:, 128:].reshape(8, RC, 128)

        if r == 0:
            keep(False).start()
            x_back(0, 1 - c).start()
        else:
            for core in (0, 1):
                x_back(r, core).start()

    def results_a(r):
        @pl.loop(0, 4)
        def _(i):
            m = pl.ds(pl.multiple_of(i * 4 * RA, 128), 4 * RA)
            part = jnp.dot(down_t[m, :], hidden[...], preferred_element_type=F32)
            pa[r, i] = part.astype(BF16).reshape(4, RA, COLS)

        for part in range(len(PARTS)):
            for sign in (1, -1):
                scatter(part, 0, sign, r).start()

    def returning(r, core, b):
        target = block_of(r, core, b)
        return remote(ret_send.at[r, core, b], ret_recv.at[me], ret_ss.at[r, core, b], ret_rs.at[me], (target, place))

    def give_back(r):
        rows = []
        for part, (r0, n) in enumerate(PARTS):
            last = land[part][3]
            total = pa[r, z, y, r0:r0 + n].astype(F32) + last[r, 0].astype(F32) + last[r, 1].astype(F32)
            rows.append(total.astype(BF16))
        whole = jnp.concatenate(rows, axis=0)
        for core in (0, 1):
            tile = whole[:, core * 128:core * 128 + 128]
            for b in (0, 1):
                lanes = slice(b * 64, b * 64 + 64)
                ret_send[r, core, b] = jnp.concatenate([tile[0:HA, lanes], tile[HA:RA, lanes]], axis=1)

                @pl.when(block_of(r, core, b) != me)
                def _():
                    returning(r, core, b).start()

                @pl.when(block_of(r, core, b) == me)
                def _():
                    ret_recv[pl.ds(me, 1)] = ret_send[r, core, pl.ds(b, 1)]

    def gather_op(step, r, part):
        if step == 0:
            if ("here", r) not in seen:
                seen.add(("here", r))
                arrive(r)
        else:
            for sign in (1, -1):
                gather(part, step - 1, sign, r, True).wait_recv()
        for sign in (1, -1):
            gather(part, step, sign, r).start()

    def scatter_op(step, r, part):
        for sign in (1, -1):
            scatter(part, step - 1, sign, r).wait_recv()
        if step == 4:
            seen.add(("summed", r, part))
            if all(("summed", r, p) in seen for p in range(len(PARTS))):
                give_back(r)
            return
        u, v = coords(part)
        got = land[part][step - 1]
        if step == 1:
            add_into(at_part(pa, r, part, LOW, wrap(v + 1, 4)), got.at[r, 0])
            add_into(at_part(pa, r, part, HIGH, wrap(v - 1, 4)), got.at[r, 1])
        elif step == 2:
            add_into(at_part(pa, r, part, ALL, v), got.at[r, 0], got.at[r, 1])
        else:
            add_into(at_part(pa, r, part, wrap(u + 1, 4), v, 0), got.at[r, 0])
            add_into(at_part(pa, r, part, wrap(u - 1, 4), v, 1), got.at[r, 1])
        for sign in (1, -1):
            scatter(part, step, sign, r).start()

    def prepare(i):
        m = pl.ds(pl.multiple_of(i * 384, 128), 384)
        wide = pl.multiple_of(i * 2 * RA, 128)
        thin = pl.multiple_of(16 * RA + i * 2 * RC, 128)
        for src, dst in ((gate_raw, gate_t), (up_raw, up_t)):
            w = src[m, :]
            dst[:, pl.ds(wide, RA)] = w[0:RA].T
            dst[:, pl.ds(wide + RA, RA)] = w[192:192 + RA].T
            dst[:, pl.ds(thin, 2 * RC)] = jnp.concatenate([w[RA:192], w[192 + RA:384]], axis=0).T
        w = down_raw[:, m].T
        down_t[pl.ds(wide, RA), :] = w[0:RA]
        down_t[pl.ds(wide + RA, RA), :] = w[192:192 + RA]
        down_t[pl.ds(thin, RC), :] = w[RA:192]
        down_t[pl.ds(thin + RC, RC), :] = w[192 + RA:384]

    seen = set()

    def loaded():
        if "loaded" not in seen:
            seen.add("loaded")
            for load in loads:
                load.wait()

    for op, *at in ORDER:
        if op == "h":
            head_step(*at)
        elif op == "pk":
            if "tokens" not in seen:
                seen.add("tokens")
                for sign in (1, -1):
                    head(5, sign, True).wait_recv()
            pick_slots(*at)
        elif op == "g":
            gather_op(*at)
        elif op == "mu":
            units(*at)
        elif op == "mc":
            results_c(*at)
        elif op == "ma":
            results_a(*at)
        elif op == "s":
            scatter_op(*at)
        elif op == "add":
            added = sum(1 for k in seen if k[0] == "add")
            seen.add(("add", *at))
            add_up(*at, added == 0, added == 3)
        elif op == "t":
            tail_step(*at)
        elif op == "prep":
            loaded()
            pl.loop(at[0] * 2, at[0] * 2 + 2)(prepare)
        elif op == "tab":
            tables()
        elif op == "own":
            own_weights()

    for sign in (1, -1):
        tail(5, sign).wait_recv()
    out_ref[RA:, :] = (tsum[z8, y].astype(F32) + y2[0].astype(F32) + y2[1].astype(F32)).astype(BF16)

    for d in range(1, 16):
        src = wrap(me + d, 16)
        remote(ret_recv.at[src], ret_recv.at[src], disp_ss.at[0], ret_rs.at[src], (src, place)).wait_recv()
    back = jnp.concatenate([ret_recv[e] for e in range(16)], axis=1)
    mixed = jnp.dot(back, w_high[...], preferred_element_type=F32) + jnp.dot(
        back, w_low[...], preferred_element_type=F32)
    out_ref[0:HA, :] = mixed[:, 0:256].astype(BF16)
    out_ref[HA:RA, :] = mixed[:, 256:512].astype(BF16)

    swap_meta().wait_send()
    for sign in (1, -1):
        for step in range(6):
            head(step, sign).wait_send()
            tail(step, sign).wait_send()
    x_out(0, 1 - c).wait_send()
    x_back(0, 1 - c).wait_send()
    for r in (1, 2, 3):
        for core in (0, 1):
            x_out(r, core).wait_send()
            x_back(r, core).wait_send()
    for d in range(1, 16):
        dispatch(d).wait_send()

    for r in range(GROUPS):
        for part in range(len(PARTS)):
            for sign in (1, -1):
                for step in range(4):
                    gather(part, step, sign, r).wait_send()
                    scatter(part, step, sign, r).wait_send()
        for core in (0, 1):
            for b in (0, 1):
                @pl.when(block_of(r, core, b) != me)
                def _():
                    returning(r, core, b).wait_send()


def body(tokens, expert_ids, pair_logits, gate_weight, up_weight, down_weight):
    vmem = pl.BlockSpec(memory_space=pltpu.VMEM)
    hbm = pl.BlockSpec(memory_space=pl.ANY)
    dma = pltpu.SemaphoreType.DMA

    def buf(*shape):
        return pltpu.VMEM(shape, BF16)

    def buf32(*shape):
        return pltpu.VMEM(shape, F32)

    landing = []
    for _, n in PARTS:
        half = (n // 2, COLS) if n % 32 == 0 else (n, 128)
        landing += [
            buf(GROUPS, 2, 2, n, COLS), buf(GROUPS, 2, 4, n, COLS), buf(GROUPS, 2, *half), buf(GROUPS, 2, n, COLS)]
    out = pl.pallas_call(
        kernel,
        out_shape=jax.ShapeDtypeStruct((192, 256), BF16),
        in_specs=[vmem, vmem, vmem, hbm, hbm, hbm],
        out_specs=vmem,
        scratch_shapes=[
            buf(3072, 512), buf(3072, 512), buf(512, 3072),
            buf(512, 3072), buf(512, 3072), buf(3072, 512),
            buf(GROUPS, 4, 4, RA, COLS), buf(GROUPS, 4, 4, RA, COLS), buf(512, COLS),
            buf(2048, 512), buf(2048, 512), buf(2048, 512),
            buf(16, HA, 128), buf(16, HA, 128), buf(GROUPS, 2, 2, HA, 128), buf(16, HA, 128),
            *landing,
            buf32(2, 8, 256), buf32(2, 16, 256), buf32(2, 16, 256),
            buf(1024, 512), buf(1024, 512), buf(1024, 512),
            buf(8, 4, RC, 256), buf(4, 2, 16, RC, 128), buf(4, 2, 16, RC, 128),
            buf(4, 2, 16, RC, 128), buf(4, 2, 16, RC, 128),
            buf32(4, 4 * RC, 512), buf(8, 4, RC, 256),
            buf(2, 2, RC, 256), buf(2, 4, RC, 256), buf(2, 4, RC, 256), buf(2, 4, RC, 256),
            buf(2, HC, 256), buf(2, RC, 256),
            dma((3,)), dma((16,)), dma((16,)), dma((GROUPS, 2, 2)), dma((16,)),
            dma((GROUPS, len(PARTS), 16)), dma((GROUPS, len(PARTS), 16)), dma((25,)), dma((25,)),
            dma((4, 2)), dma((4, 2)), dma((4, 2)), dma((4, 2)), dma((2,)),
        ],
        compiler_params=pltpu.CompilerParams(
            collective_id=0, has_side_effects=True, vmem_limit_bytes=60 * 2**20),
        cost_estimate=pl.CostEstimate(flops=9_700_000_000, bytes_accessed=10_000_000, transcendentals=524288),
    )(tokens.T, expert_ids.T, pair_logits.T, gate_weight[0], up_weight[0], down_weight[0])
    return out.T


def solution(mesh):
    in_specs = (
        P("expert", "split"),
        P("expert", None),
        P("expert", None),
        P("expert", None, "split"),
        P("expert", None, "split"),
        P("expert", "split", None),
    )
    return jax.shard_map(body, mesh=mesh, in_specs=in_specs, out_specs=P("expert", "split"), check_vma=False)
```

time: 294 us -> 130 us (0.44)
  waiting for transfers between devices: 214 us -> 0 us
  Pallas kernels: 0 us -> 128 us
  matrix products: 22.6 us -> 0 us
  blocking collectives: 17.2 us -> 0 us
  local copies, waits for them, and re-layouts: 15.3 us -> 1.54 us
  between operations: 13.5 us -> 0.01 us
  starting transfers between devices: 5.48 us -> 0 us
  other arithmetic: 5.22 us -> 0 us
    pallas_call x0 -> x1, Pallas kernels: none -> 128 us  [body(): pl.pallas_call(kernel, out_shape=jax.ShapeDtypeStruct((192, 256), BF16),...]
    reduce_scatter x1 -> x0, waiting for transfers between devices: 113 us -> none  [body(): lax.psum_scatter(terms.astype(jnp.bfloat16), 'split', scatter_dimension=1...]
    all_gather x1 -> x0, waiting for transfers between devices: 91.2 us -> none  [body(): piece = lax.all_gather(arrived, 'split', axis=1, tiled=True)]
    dot_general x3 -> x0, matrix products: 22.6 us -> none  [the longest x1 12.5 us: body(): terms = jnp.dot(hidden, w_down, preferred_element_type=jnp.float32)]
    all_to_all x1 -> x0, blocking collectives: 17.2 us -> none  [body(): lax.all_to_all(sending, 'expert', split_axis=0, concat_axis=0, tiled=True)]
    all_to_all x1 -> x0, waiting for transfers between devices: 9.38 us -> none  [body(): lax.all_to_all(result.reshape(experts, capacity, narrow).astype(jnp.bfloa...]
    gather x2 -> x0, local copies, waits for them, and re-layouts: 5.6 us -> none  [body(): picked = returned[dest] * mix[:, None]]
    all_to_all x1 -> x0, starting transfers between devices: 5.43 us -> none  [body(): lax.all_to_all(result.reshape(experts, capacity, narrow).astype(jnp.bfloa...]
  transfers between devices with their start and end apart: 3 -> 0, of which waited for: 3 -> 0; matrix products, arithmetic and copies ran while one was open for 0% -> 0% of each run, Pallas kernels for 0% -> 0%
where the time goes in v2:
time: 130 us
  Pallas kernels  128 us (98%)
  local copies, waits for them, and re-layouts  1.54 us (1%)
    pallas_call x1, Pallas kernels, body(): pl.pallas_call(kernel, out_shape=jax.ShapeDtypeStruct((192, 256), BF16),...  128 us

profile of v2, /device:TPU:1, one launch (start us, length us, event | category | flops | bytes accessed | tf_op | source)
XLA Modules:
  0.0 129.6 jit_solution(14631952875895310650)
XLA Ops:
  0.0 128.1 %shard_map.64 = bf16[192,256]{1,0:T(8,128)(2,1)} custom-call(bf16[192,256]{1,0:T(8,128)(2,1)} %bitcast.11, s32[2,256]{1,0:T(2,128)} %bitcast.12, f32[2,256]{1,0:T(2,128)} %bitcast.13, bf16[3072,512]{1,0:T(8,128)(2,1)} %bitcast.8, bf16[3072,512]{1,0:T(8,128)(2,1)} %bitcast.9, bf16[512,3072]{1,0:T(8,128)(2,1)} %bitcast.10), custom_call_target="tpu_custom_call" | custom-call | flops 9699999744 | bytes 10000000 | tf_op jit(solution)/shard_map/pallas_call | solution.py:593
  128.1 1.5 %copy.8 = bf16[256,192]{0,1:T(8,128)(2,1)} copy(bf16[256,192]{0,1:T(8,128)(2,1)} %bitcast.7) | data formatting | bytes 196608

commit v3 on v2

--- a/solution.py
+++ b/solution.py
@@ -18,18 +18,18 @@
 RC = 64
 HA, HC = RA // 2, RC // 2
 ORDER = (
-    ("g", 0, 0, 0), ("h", 1), ("h", 2), ("g", 1, 0, 0), ("g", 0, 1, 0), ("g", 2, 0, 0),
-    ("h", 3), ("prep", 3), ("prep", 0), ("prep", 1), ("tab",), ("g", 1, 1, 0),
-    ("h", 4), ("g", 2, 1, 0), ("g", 0, 3, 0), ("h", 5), ("g", 3, 0, 0), ("g", 1, 3, 0),
-    ("pk", 1), ("g", 3, 1, 0), ("pk", 3), ("g", 2, 3, 0), ("prep", 2), ("g", 0, 2, 0),
-    ("pk", 0), ("mu", 0), ("mc", 0), ("ma", 0), ("g", 1, 2, 0), ("pk", 2),
-    ("g", 2, 2, 0), ("add", 0), ("g", 3, 3, 0), ("mu", 1), ("mc", 1), ("ma", 1),
-    ("mu", 3), ("g", 3, 2, 0), ("mc", 3), ("s", 1, 0, 0), ("ma", 3), ("mu", 2),
-    ("s", 1, 1, 0), ("mc", 2), ("s", 2, 0, 0), ("s", 3, 0, 0), ("s", 1, 3, 0), ("ma", 2),
-    ("s", 2, 1, 0), ("s", 4, 0, 0), ("s", 3, 1, 0), ("add", 1), ("add", 3), ("add", 2),
-    ("t", 0), ("s", 2, 3, 0), ("t", 1), ("s", 1, 2, 0), ("s", 3, 3, 0), ("s", 4, 1, 0),
-    ("t", 2), ("s", 4, 3, 0), ("s", 2, 2, 0), ("t", 3), ("s", 3, 2, 0), ("own",),
-    ("t", 4), ("s", 4, 2, 0), ("t", 5),
+    ("h", 1), ("own",), ("g", 0, 0, 0), ("prep", 2), ("g", 0, 1, 0), ("h", 2),
+    ("g", 1, 0, 0), ("g", 1, 1, 0), ("h", 3), ("g", 2, 0, 0), ("g", 0, 3, 0), ("prep", 0),
+    ("prep", 3), ("h", 4), ("g", 2, 1, 0), ("tab",), ("g", 0, 2, 0), ("h", 5),
+    ("g", 1, 3, 0), ("g", 3, 0, 0), ("g", 1, 2, 0), ("g", 3, 1, 0), ("pk", 3), ("pk", 1),
+    ("pk", 0), ("g", 2, 3, 0), ("prep", 1), ("mu", 0), ("g", 2, 2, 0), ("g", 3, 3, 0),
+    ("pk", 2), ("mc", 0), ("ma", 0), ("mu", 1), ("mc", 1), ("ma", 1),
+    ("g", 3, 2, 0), ("mu", 3), ("mc", 3), ("s", 1, 0, 0), ("s", 1, 1, 0), ("ma", 3),
+    ("mu", 2), ("mc", 2), ("ma", 2), ("s", 2, 0, 0), ("s", 2, 1, 0), ("add", 3),
+    ("s", 1, 3, 0), ("s", 3, 0, 0), ("s", 1, 2, 0), ("add", 0), ("s", 3, 1, 0), ("add", 1),
+    ("add", 2), ("t", 0), ("s", 2, 3, 0), ("s", 4, 1, 0), ("t", 1), ("s", 2, 2, 0),
+    ("t", 2), ("s", 3, 3, 0), ("t", 3), ("s", 3, 2, 0), ("t", 4), ("s", 4, 3, 0),
+    ("t", 5), ("s", 4, 2, 0), ("s", 4, 0, 0),
 )
 FAR = (0, 1, 3, 2)
 
@@ -152,6 +152,11 @@
         one = one_hot(slot[e:e + 1, :])
         place_two(sel, e * 128, one, one)
 
+    pl.semaphore_wait(barrier, 20)
+    swap_meta().start()
+    for sign in (1, -1):
+        head(0, sign).start()
+
     halves = jnp.concatenate([tok[0:HA, :], tok[HA:RA, :]], axis=1)
     for e in range(16):
         disp_send[e] = lax.dot_general(
@@ -164,10 +169,6 @@
         target = wrap(x + FAR[step], 4) * 4 + wrap(me - x * 4 + inner, 4)
         return remote(disp_send.at[target], disp_recv.at[me], disp_ss.at[d], disp_rs.at[me], (target, place))
 
-    pl.semaphore_wait(barrier, 20)
-    swap_meta().start()
-    for sign in (1, -1):
-        head(0, sign).start()
     for d in range(1, 16):
         dispatch(d).start()
 
@@ -479,19 +480,52 @@
             scatter(part, step, sign, r).start()
 
     def prepare(i):
-        m = pl.ds(pl.multiple_of(i * 384, 128), 384)
-        wide = pl.multiple_of(i * 2 * RA, 128)
-        thin = pl.multiple_of(16 * RA + i * 2 * RC, 128)
+        m = pl.ds(pl.multiple_of(i * 768, 128), 768)
+        wide = pl.ds(pl.multiple_of(i * 4 * RA, 128), 4 * RA)
+        thin = pl.ds(pl.multiple_of(16 * RA + i * 4 * RC, 128), 4 * RC)
+
+        def sorted_rows(w):
+            return (jnp.concatenate([w[n * 192:n * 192 + RA] for n in range(4)], axis=0),
+                    jnp.concatenate([w[n * 192 + RA:n * 192 + 192] for n in range(4)], axis=0))
+
         for src, dst in ((gate_raw, gate_t), (up_raw, up_t)):
-            w = src[m, :]
-            dst[:, pl.ds(wide, RA)] = w[0:RA].T
-            dst[:, pl.ds(wide + RA, RA)] = w[192:192 + RA].T
-            dst[:, pl.ds(thin, 2 * RC)] = jnp.concatenate([w[RA:192], w[192 + RA:384]], axis=0).T
-        w = down_raw[:, m].T
-        down_t[pl.ds(wide, RA), :] = w[0:RA]
-        down_t[pl.ds(wide + RA, RA), :] = w[192:192 + RA]
-        down_t[pl.ds(thin, RC), :] = w[RA:192]
-        down_t[pl.ds(thin + RC, RC), :] = w[192 + RA:384]
+            first, second = sorted_rows(src[m, :])
+            dst[:, wide] = first.T
+            dst[:, thin] = second.T
+        first, second = sorted_rows(down_raw[:, m].T)
+        down_t[wide, :] = first
+        down_t[thin, :] = second
+
+    def gather_sent():
+        swap_meta().wait_send()
+        for sign in (1, -1):
+            for step in range(6):
+                head(step, sign).wait_send()
+        x_out(0, 1 - c).wait_send()
+        for r in (1, 2, 3):
+            for core in (0, 1):
+                x_out(r, core).wait_send()
+        for d in range(1, 16):
+            dispatch(d).wait_send()
+        for r in range(GROUPS):
+            for part in range(len(PARTS)):
+                for sign in (1, -1):
+                    for step in range(4):
+                        gather(part, step, sign, r).wait_send()
+
+    def sums_sent():
+        for sign in (1, -1):
+            for step in range(5):
+                tail(step, sign).wait_send()
+        x_back(0, 1 - c).wait_send()
+        for r in (1, 2, 3):
+            for core in (0, 1):
+                x_back(r, core).wait_send()
+        for r in range(GROUPS):
+            for part in range(len(PARTS)):
+                for sign in (1, -1):
+                    for step in range(4):
+                        scatter(part, step, sign, r).wait_send()
 
     seen = set()
 
@@ -526,18 +560,17 @@
             add_up(*at, added == 0, added == 3)
         elif op == "t":
             tail_step(*at)
+            if at[0] == 2:
+                gather_sent()
         elif op == "prep":
             loaded()
-            pl.loop(at[0] * 2, at[0] * 2 + 2)(prepare)
+            prepare(at[0])
         elif op == "tab":
             tables()
         elif op == "own":
             own_weights()
 
-    for sign in (1, -1):
-        tail(5, sign).wait_recv()
-    out_ref[RA:, :] = (tsum[z8, y].astype(F32) + y2[0].astype(F32) + y2[1].astype(F32)).astype(BF16)
-
+    sums_sent()
     for d in range(1, 16):
         src = wrap(me + d, 16)
         remote(ret_recv.at[src], ret_recv.at[src], disp_ss.at[0], ret_rs.at[src], (src, place)).wait_recv()
@@ -547,26 +580,13 @@
     out_ref[0:HA, :] = mixed[:, 0:256].astype(BF16)
     out_ref[HA:RA, :] = mixed[:, 256:512].astype(BF16)
 
-    swap_meta().wait_send()
     for sign in (1, -1):
-        for step in range(6):
-            head(step, sign).wait_send()
-            tail(step, sign).wait_send()
-    x_out(0, 1 - c).wait_send()
-    x_back(0, 1 - c).wait_send()
-    for r in (1, 2, 3):
-        for core in (0, 1):
-            x_out(r, core).wait_send()
-            x_back(r, core).wait_send()
-    for d in range(1, 16):
-        dispatch(d).wait_send()
-
+        tail(5, sign).wait_recv()
+    out_ref[RA:, :] = (tsum[z8, y].astype(F32) + y2[0].astype(F32) + y2[1].astype(F32)).astype(BF16)
+
+    for sign in (1, -1):
+        tail(5, sign).wait_send()
     for r in range(GROUPS):
-        for part in range(len(PARTS)):
-            for sign in (1, -1):
-                for step in range(4):
-                    gather(part, step, sign, r).wait_send()
-                    scatter(part, step, sign, r).wait_send()
         for core in (0, 1):
             for b in (0, 1):
                 @pl.when(block_of(r, core, b) != me)

time: 130 us -> 127 us (0.977)
  Pallas kernels: 128 us -> 125 us
    pallas_call x1, Pallas kernels: 128 us -> 125 us  [body(): pl.pallas_call(kernel, out_shape=jax.ShapeDtypeStruct((192, 256), BF16),...]
where the time goes in v3:
time: 127 us
  Pallas kernels  125 us (98%)
  local copies, waits for them, and re-layouts  1.54 us (1%)
    pallas_call x1, Pallas kernels, body(): pl.pallas_call(kernel, out_shape=jax.ShapeDtypeStruct((192, 256), BF16),...  125 us

profile of v3, /device:TPU:1, one launch (start us, length us, event | category | flops | bytes accessed | tf_op | source)
XLA Modules:
  0.0 126.5 jit_solution(15878409422562306614)
XLA Ops:
  0.0 125.0 %shard_map.64 = bf16[192,256]{1,0:T(8,128)(2,1)} custom-call(bf16[192,256]{1,0:T(8,128)(2,1)} %bitcast.11, s32[2,256]{1,0:T(2,128)} %bitcast.12, f32[2,256]{1,0:T(2,128)} %bitcast.13, bf16[3072,512]{1,0:T(8,128)(2,1)} %bitcast.8, bf16[3072,512]{1,0:T(8,128)(2,1)} %bitcast.9, bf16[512,3072]{1,0:T(8,128)(2,1)} %bitcast.10), custom_call_target="tpu_custom_call" | custom-call | flops 9699999744 | bytes 10000000 | tf_op jit(solution)/shard_map/pallas_call | solution.py:613
  125.0 1.5 %copy.8 = bf16[256,192]{0,1:T(8,128)(2,1)} copy(bf16[256,192]{0,1:T(8,128)(2,1)} %bitcast.7) | data formatting | bytes 196608

commit v4 on v3

--- a/solution.py
+++ b/solution.py
@@ -13,23 +13,28 @@
 
 COLS = 256
 GROUPS = 4
-PARTS = ((0, 128),)
-RA = 128
-RC = 64
+PARTS = ((0, 128), (128, 32))
+RA = 160
+RC = 32
 HA, HC = RA // 2, RC // 2
 ORDER = (
-    ("h", 1), ("own",), ("g", 0, 0, 0), ("prep", 2), ("g", 0, 1, 0), ("h", 2),
-    ("g", 1, 0, 0), ("g", 1, 1, 0), ("h", 3), ("g", 2, 0, 0), ("g", 0, 3, 0), ("prep", 0),
-    ("prep", 3), ("h", 4), ("g", 2, 1, 0), ("tab",), ("g", 0, 2, 0), ("h", 5),
-    ("g", 1, 3, 0), ("g", 3, 0, 0), ("g", 1, 2, 0), ("g", 3, 1, 0), ("pk", 3), ("pk", 1),
-    ("pk", 0), ("g", 2, 3, 0), ("prep", 1), ("mu", 0), ("g", 2, 2, 0), ("g", 3, 3, 0),
-    ("pk", 2), ("mc", 0), ("ma", 0), ("mu", 1), ("mc", 1), ("ma", 1),
-    ("g", 3, 2, 0), ("mu", 3), ("mc", 3), ("s", 1, 0, 0), ("s", 1, 1, 0), ("ma", 3),
-    ("mu", 2), ("mc", 2), ("ma", 2), ("s", 2, 0, 0), ("s", 2, 1, 0), ("add", 3),
-    ("s", 1, 3, 0), ("s", 3, 0, 0), ("s", 1, 2, 0), ("add", 0), ("s", 3, 1, 0), ("add", 1),
-    ("add", 2), ("t", 0), ("s", 2, 3, 0), ("s", 4, 1, 0), ("t", 1), ("s", 2, 2, 0),
-    ("t", 2), ("s", 3, 3, 0), ("t", 3), ("s", 3, 2, 0), ("t", 4), ("s", 4, 3, 0),
-    ("t", 5), ("s", 4, 2, 0), ("s", 4, 0, 0),
+    ("tab",), ("prep", 0), ("h", 1), ("g", 0, 0, 0), ("g", 0, 1, 1), ("g", 0, 2, 0),
+    ("g", 0, 0, 1), ("g", 1, 0, 1), ("g", 1, 0, 0), ("g", 0, 2, 1), ("prep", 1), ("h", 2),
+    ("g", 0, 1, 0), ("g", 2, 0, 0), ("g", 1, 2, 0), ("h", 3), ("g", 0, 3, 1), ("g", 1, 1, 0),
+    ("g", 0, 3, 0), ("g", 2, 2, 0), ("h", 4), ("g", 1, 3, 1), ("g", 1, 1, 1), ("g", 2, 0, 1),
+    ("g", 1, 2, 1), ("g", 3, 0, 0), ("h", 5), ("prep", 3), ("g", 2, 1, 0), ("g", 1, 3, 0),
+    ("prep", 2), ("g", 3, 0, 1), ("pk", 0), ("pk", 2), ("g", 2, 1, 1), ("pk", 3),
+    ("g", 2, 3, 0), ("pk", 1), ("g", 2, 3, 1), ("mu", 0), ("g", 3, 1, 1), ("mc", 0),
+    ("g", 2, 2, 1), ("g", 3, 1, 0), ("g", 3, 3, 0), ("g", 3, 3, 1), ("ma", 0), ("add", 0),
+    ("mu", 1), ("g", 3, 2, 0), ("mc", 1), ("ma", 1), ("mu", 3), ("g", 3, 2, 1),
+    ("mc", 3), ("s", 1, 0, 1), ("ma", 3), ("s", 1, 1, 0), ("s", 1, 1, 1), ("mu", 2),
+    ("mc", 2), ("add", 1), ("s", 1, 0, 0), ("s", 1, 3, 1), ("s", 2, 1, 0), ("ma", 2),
+    ("add", 3), ("s", 1, 3, 0), ("own",), ("add", 2), ("t", 0), ("s", 2, 0, 1),
+    ("s", 2, 1, 1), ("s", 3, 1, 0), ("t", 1), ("s", 2, 3, 1), ("s", 1, 2, 1), ("s", 1, 2, 0),
+    ("t", 2), ("s", 3, 3, 1), ("s", 2, 3, 0), ("s", 3, 1, 1), ("s", 2, 2, 1), ("s", 2, 0, 0),
+    ("t", 3), ("s", 3, 0, 1), ("s", 3, 3, 0), ("s", 2, 2, 0), ("s", 3, 2, 1), ("s", 4, 3, 1),
+    ("s", 4, 2, 1), ("s", 3, 0, 0), ("s", 4, 1, 1), ("t", 4), ("s", 3, 2, 0), ("s", 4, 0, 0),
+    ("s", 4, 1, 0), ("s", 4, 0, 1), ("s", 4, 3, 0), ("s", 4, 2, 0), ("t", 5),
 )
 FAR = (0, 1, 3, 2)
 
@@ -42,7 +47,7 @@
     tok_ref, ids_ref, logit_ref, gate_hbm, up_hbm, down_hbm, out_ref,
     gate_raw, up_raw, down_raw, gate_t, up_t, down_t,
     xa, pa, hidden, sel, w_high, w_low,
-    disp_send, disp_recv, ret_send, ret_recv, a1, a2, a3, a4,
+    disp_send, disp_recv, ret_send, ret_recv, a1, a2, a3, a4, b1, b2, b3, b4,
     meta, slots, mixes, sel_c, wc_high, wc_low,
     raw, xs, xc, pc, tr, acc, tsum, z1, z2, z3, z4, y1, y2,
     weight_sem, disp_ss, disp_rs, ret_ss, ret_rs, ss, rs, cs, cr, xss, xrs, tss, trs, local_sem,
@@ -306,7 +311,7 @@
         for sign in (1, -1):
             tail(step, sign).start()
 
-    land = ((a1, a2, a3, a4),)
+    land = ((a1, a2, a3, a4), (b1, b2, b3, b4))
 
     def at_part(ref, r, part, i, j, half=None):
         r0, n = PARTS[part]

time: 127 us -> 122 us (0.961)
  Pallas kernels: 125 us -> 120 us
    pallas_call x1, Pallas kernels: 125 us -> 120 us  [body(): pl.pallas_call(kernel, out_shape=jax.ShapeDtypeStruct((192, 256), BF16),...]
where the time goes in v4:
time: 122 us
  Pallas kernels  120 us (98%)
  local copies, waits for them, and re-layouts  1.54 us (1%)
    pallas_call x1, Pallas kernels, body(): pl.pallas_call(kernel, out_shape=jax.ShapeDtypeStruct((192, 256), BF16),...  120 us

profile of v4, /device:TPU:1, one launch (start us, length us, event | category | flops | bytes accessed | tf_op | source)
XLA Modules:
  0.0 121.5 jit_solution(7843673292260710997)
XLA Ops:
  0.0 120.0 %shard_map.64 = bf16[192,256]{1,0:T(8,128)(2,1)} custom-call(bf16[192,256]{1,0:T(8,128)(2,1)} %bitcast.11, s32[2,256]{1,0:T(2,128)} %bitcast.12, f32[2,256]{1,0:T(2,128)} %bitcast.13, bf16[3072,512]{1,0:T(8,128)(2,1)} %bitcast.8, bf16[3072,512]{1,0:T(8,128)(2,1)} %bitcast.9, bf16[512,3072]{1,0:T(8,128)(2,1)} %bitcast.10), custom_call_target="tpu_custom_call" | custom-call | flops 9699999744 | bytes 10000000 | tf_op jit(solution)/shard_map/pallas_call | solution.py:618
  120.0 1.5 %copy.8 = bf16[256,192]{0,1:T(8,128)(2,1)} copy(bf16[256,192]{0,1:T(8,128)(2,1)} %bitcast.7) | data formatting | bytes 196608

commit v5 on v4

--- a/solution.py
+++ b/solution.py
@@ -18,23 +18,23 @@
 RC = 32
 HA, HC = RA // 2, RC // 2
 ORDER = (
-    ("tab",), ("prep", 0), ("h", 1), ("g", 0, 0, 0), ("g", 0, 1, 1), ("g", 0, 2, 0),
-    ("g", 0, 0, 1), ("g", 1, 0, 1), ("g", 1, 0, 0), ("g", 0, 2, 1), ("prep", 1), ("h", 2),
-    ("g", 0, 1, 0), ("g", 2, 0, 0), ("g", 1, 2, 0), ("h", 3), ("g", 0, 3, 1), ("g", 1, 1, 0),
-    ("g", 0, 3, 0), ("g", 2, 2, 0), ("h", 4), ("g", 1, 3, 1), ("g", 1, 1, 1), ("g", 2, 0, 1),
-    ("g", 1, 2, 1), ("g", 3, 0, 0), ("h", 5), ("prep", 3), ("g", 2, 1, 0), ("g", 1, 3, 0),
-    ("prep", 2), ("g", 3, 0, 1), ("pk", 0), ("pk", 2), ("g", 2, 1, 1), ("pk", 3),
-    ("g", 2, 3, 0), ("pk", 1), ("g", 2, 3, 1), ("mu", 0), ("g", 3, 1, 1), ("mc", 0),
-    ("g", 2, 2, 1), ("g", 3, 1, 0), ("g", 3, 3, 0), ("g", 3, 3, 1), ("ma", 0), ("add", 0),
-    ("mu", 1), ("g", 3, 2, 0), ("mc", 1), ("ma", 1), ("mu", 3), ("g", 3, 2, 1),
-    ("mc", 3), ("s", 1, 0, 1), ("ma", 3), ("s", 1, 1, 0), ("s", 1, 1, 1), ("mu", 2),
-    ("mc", 2), ("add", 1), ("s", 1, 0, 0), ("s", 1, 3, 1), ("s", 2, 1, 0), ("ma", 2),
-    ("add", 3), ("s", 1, 3, 0), ("own",), ("add", 2), ("t", 0), ("s", 2, 0, 1),
-    ("s", 2, 1, 1), ("s", 3, 1, 0), ("t", 1), ("s", 2, 3, 1), ("s", 1, 2, 1), ("s", 1, 2, 0),
-    ("t", 2), ("s", 3, 3, 1), ("s", 2, 3, 0), ("s", 3, 1, 1), ("s", 2, 2, 1), ("s", 2, 0, 0),
-    ("t", 3), ("s", 3, 0, 1), ("s", 3, 3, 0), ("s", 2, 2, 0), ("s", 3, 2, 1), ("s", 4, 3, 1),
-    ("s", 4, 2, 1), ("s", 3, 0, 0), ("s", 4, 1, 1), ("t", 4), ("s", 3, 2, 0), ("s", 4, 0, 0),
-    ("s", 4, 1, 0), ("s", 4, 0, 1), ("s", 4, 3, 0), ("s", 4, 2, 0), ("t", 5),
+    ("h", 1), ("g", 0, 0, 0), ("g", 0, 1, 1), ("g", 0, 3, 0), ("g", 1, 0, 0), ("tab",),
+    ("g", 0, 2, 1), ("h", 2), ("g", 1, 3, 0), ("prep", 2), ("g", 0, 0, 1), ("g", 1, 2, 1),
+    ("g", 0, 1, 0), ("g", 2, 0, 0), ("g", 1, 0, 1), ("h", 3), ("g", 2, 3, 0), ("g", 0, 3, 1),
+    ("g", 0, 2, 0), ("g", 1, 1, 0), ("h", 4), ("g", 1, 1, 1), ("g", 2, 0, 1), ("g", 3, 0, 0),
+    ("h", 5), ("g", 2, 1, 0), ("g", 1, 2, 0), ("g", 2, 2, 1), ("pk", 1), ("g", 1, 3, 1),
+    ("prep", 1), ("pk", 3), ("g", 3, 0, 1), ("g", 2, 2, 0), ("g", 2, 1, 1), ("prep", 3),
+    ("pk", 0), ("pk", 2), ("g", 3, 1, 0), ("prep", 0), ("g", 2, 3, 1), ("mu", 0),
+    ("g", 3, 1, 1), ("g", 3, 3, 0), ("mc", 0), ("g", 3, 3, 1), ("ma", 0), ("g", 3, 2, 0),
+    ("mu", 1), ("g", 3, 2, 1), ("mc", 1), ("ma", 1), ("mu", 3), ("s", 1, 0, 1),
+    ("mc", 3), ("ma", 3), ("s", 1, 0, 0), ("mu", 2), ("s", 1, 1, 1), ("mc", 2),
+    ("s", 1, 3, 1), ("ma", 2), ("s", 1, 1, 0), ("add", 0), ("add", 1), ("add", 3),
+    ("s", 2, 0, 0), ("add", 2), ("s", 1, 2, 1), ("s", 2, 0, 1), ("s", 1, 3, 0), ("t", 0),
+    ("s", 2, 3, 1), ("s", 3, 0, 0), ("s", 2, 1, 1), ("t", 1), ("s", 2, 1, 0), ("s", 2, 2, 1),
+    ("s", 1, 2, 0), ("t", 2), ("s", 2, 3, 0), ("s", 3, 1, 0), ("s", 3, 3, 1), ("s", 3, 2, 1),
+    ("s", 2, 2, 0), ("s", 3, 3, 0), ("s", 4, 3, 1), ("s", 4, 2, 1), ("s", 4, 0, 0), ("t", 3),
+    ("s", 4, 1, 0), ("s", 3, 2, 0), ("s", 3, 1, 1), ("t", 4), ("s", 4, 1, 1), ("s", 4, 3, 0),
+    ("s", 3, 0, 1), ("t", 5), ("s", 4, 2, 0), ("s", 4, 0, 1), ("own",),
 )
 FAR = (0, 1, 3, 2)
 

time: 122 us -> 119 us (0.975)
  Pallas kernels: 120 us -> 117 us
    pallas_call x1, Pallas kernels: 120 us -> 117 us  [body(): pl.pallas_call(kernel, out_shape=jax.ShapeDtypeStruct((192, 256), BF16),...]
where the time goes in v5:
time: 119 us
  Pallas kernels  117 us (98%)
  local copies, waits for them, and re-layouts  1.54 us (1%)
    pallas_call x1, Pallas kernels, body(): pl.pallas_call(kernel, out_shape=jax.ShapeDtypeStruct((192, 256), BF16),...  117 us

profile of v5, /device:TPU:1, one launch (start us, length us, event | category | flops | bytes accessed | tf_op | source)
XLA Modules:
  0.0 118.5 jit_solution(8643616687719055389)
XLA Ops:
  0.0 117.0 %shard_map.64 = bf16[192,256]{1,0:T(8,128)(2,1)} custom-call(bf16[192,256]{1,0:T(8,128)(2,1)} %bitcast.11, s32[2,256]{1,0:T(2,128)} %bitcast.12, f32[2,256]{1,0:T(2,128)} %bitcast.13, bf16[3072,512]{1,0:T(8,128)(2,1)} %bitcast.8, bf16[3072,512]{1,0:T(8,128)(2,1)} %bitcast.9, bf16[512,3072]{1,0:T(8,128)(2,1)} %bitcast.10), custom_call_target="tpu_custom_call" | custom-call | flops 9699999744 | bytes 10000000 | tf_op jit(solution)/shard_map/pallas_call | solution.py:618
  117.0 1.5 %copy.8 = bf16[256,192]{0,1:T(8,128)(2,1)} copy(bf16[256,192]{0,1:T(8,128)(2,1)} %bitcast.7) | data formatting | bytes 196608
